TPU v7x, 32 devices: a whole 2x2x4 slice. The times are simulated.
32 devices in a mesh: groups: 2 (over y), ctx: 4 (over z), stream: 2 (over x), head: 2 (over core).
Axes of the slice: x: 2, y: 2, z: 4, core: 2. Of those that a mesh axis runs over, the one named last changes fastest.
Arguments:
- queries: bfloat16 [4, 2048, 12, 128], P(('groups', 'stream'), 'ctx', 'head'), parts along dimension 0, may hold values from -9 to 9
- new_keys: bfloat16 [4, 2048, 4, 128], P(('groups', 'stream'), 'ctx', 'head'), parts along dimension 0, may hold values from -4 to 4
- new_values: bfloat16 [4, 2048, 4, 128], P(('groups', 'stream'), 'ctx', 'head'), parts along dimension 0, may hold values from -6 to 6
- cache_keys: bfloat16 [4, 6144, 4, 128], P(('groups', 'stream'), 'ctx', 'head'), parts along dimension 0, may hold values from -6 to 6
- cache_values: bfloat16 [4, 6144, 4, 128], P(('groups', 'stream'), 'ctx', 'head'), parts along dimension 0, may hold values from -6 to 6
- block_slot: int32 [4, 48], P(('groups', 'stream')), parts along dimension 0, may hold values from 0 to 47, as said below
- block_lists: int32 [4, 4, 4, 32], P(('groups', 'stream'), 'head'), parts along dimension 0, may hold values from 0 to 47, as said below
- frame_pos: int32 [4], P(('groups', 'stream')), parts along dimension 0, may hold values from 4609 to 6144, as said below
Outputs:
- attended: bfloat16 [4, 2048, 12, 128], P(('groups', 'stream'), 'ctx', 'head'), parts along dimension 0
There are 2 independent parts, one for each index of `groups`. A program takes and returns all parts, laid end to end along the dimension named above; each array names one. Nothing has to cross between parts.
Inputs may be any that keep to these rules, and one draw needn't show every extreme that they name: `block_slot`: each stream's row names every slot once; slot j lies on index j // 12 of ctx; logical blocks whose numbers agree modulo 48 / 12 lie on one index of ctx, and blocks of different residues on different indices. `block_lists`: each list holds 32 distinct logical blocks: first the 4 most recent blocks that hold cached tokens of the stream, ascending, the last being the block of position frame_pos - 1; then 28 older blocks. At most 8 blocks of a list lie on one index of ctx, and exactly 8 on the index that holds the list's last recent block. `frame_pos`: stream 0 has a full cache.
All inputs are finite; a program needn't handle non-finite values.
Results may differ from a plain program's by a relative error of at most 0.015.
Values may be sent and summed in bfloat16 or wider, within the bound.
A program may use at most 192 MiB of HBM per device.

v0:
```python
import functools

import jax
import jax.numpy as jnp
from jax import lax
from jax.experimental import pallas as pl
from jax.experimental.pallas import tpu as pltpu
from jax.sharding import PartitionSpec as P

BLOCK = 128
FLOOR = -1e30
LOG2E = 1.4426950408889634
MESH = pl.DeviceIdType.MESH


def lookup(slot_table, indices):
    entries = jnp.arange(slot_table.shape[0], dtype=jnp.int32)
    return jnp.sum(jnp.where(indices[..., None] == entries, slot_table, 0), axis=-1)


def local_blocks(slot_table, lists, filled, own_index, cb_dev, capacity):
    slot_entry = lookup(slot_table, lists)
    mine = (slot_entry // cb_dev) == own_index
    count = lists.shape[-1]
    positions = jnp.arange(count, dtype=jnp.int32)
    earlier = positions[:, None] > positions[None, :]
    rank = jnp.sum((mine[..., None, :] & earlier).astype(jnp.int32), axis=-1)
    slot_ids = jnp.arange(capacity, dtype=jnp.int32)
    matched = mine[..., None] & (rank[..., None] == slot_ids)
    rows = jnp.clip(filled - lists * BLOCK, 0, BLOCK)
    slots = jnp.sum(jnp.where(matched, (slot_entry % cb_dev)[..., None], 0), axis=2)
    limits = jnp.sum(jnp.where(matched, rows[..., None], 0), axis=2)
    return slots, limits


def kernel(
    n, slots_ref, limits_ref, q_ref, kn_ref, vn_ref, kc_ref, vc_ref, out_ref,
    qbuf, rin, lin, rout, lout, acc, lacc, qs, qr, rs, rr, ls, lr,
):
    heads, tok, hd = q_ref.shape
    group = heads // kn_ref.shape[0]
    capacity = slots_ref.shape[2]
    me = lax.axis_index("ctx")
    scale = LOG2E * hd ** -0.5

    barrier = pltpu.get_barrier_semaphore()

    @pl.when(me > 0)
    def _():
        pl.semaphore_signal(barrier, inc=1, device_id={"ctx": me - 1}, device_id_type=MESH)

    @pl.when(me < n - 1)
    def _():
        pl.semaphore_signal(barrier, inc=1, device_id={"ctx": me + 1}, device_id_type=MESH)

    peers = jnp.where(me > 0, 1, 0) + jnp.where(me < n - 1, 1, 0)
    pl.semaphore_wait(barrier, peers)

    def q_copy(src, way, t, h):
        return pltpu.make_async_remote_copy(
            src_ref=src, dst_ref=qbuf.at[t, h], send_sem=qs.at[way, t, h], recv_sem=qr.at[t, h],
            device_id={"ctx": me + 1 - 2 * way}, device_id_type=MESH,
        )

    def r_copies(way, t, h):
        peer = {"ctx": me + 1 - 2 * way}
        return (
            pltpu.make_async_remote_copy(
                src_ref=rout.at[t, h], dst_ref=rin.at[way, t, h], send_sem=rs.at[t, h],
                recv_sem=rr.at[way, t, h], device_id=peer, device_id_type=MESH,
            ),
            pltpu.make_async_remote_copy(
                src_ref=lout.at[t, h], dst_ref=lin.at[way, t, h], send_sem=ls.at[t, h],
                recv_sem=lr.at[way, t, h], device_id=peer, device_id_type=MESH,
            ),
        )

    def can_send(way):
        return me < n - 1 if way == 0 else me > 0

    @pl.loop(0, heads)
    def _(h):
        for way in (0, 1):
            @pl.when(can_send(way))
            def _():
                q_copy(q_ref.at[h], way, me, h).start()

    def partial(q, t, h):
        g = h // group
        rows = lax.broadcasted_iota(jnp.int32, (BLOCK, tok), 0)
        nt = (((1,), (1,)), ((), ()))
        pieces = [
            ([lax.dot_general(kn_ref[g], q, nt, preferred_element_type=jnp.float32)], vn_ref[g])
        ]
        for first in range(0, capacity, 4):
            ids = range(first, min(first + 4, capacity))
            where = [slots_ref[g, t, c] for c in ids]
            keys = jnp.concatenate([kc_ref[g, w] for w in where], axis=0)
            values = jnp.concatenate([vc_ref[g, w] for w in where], axis=1)
            s = lax.dot_general(keys, q, nt, preferred_element_type=jnp.float32)
            parts = []
            for k, c in enumerate(ids):
                block = s[k * BLOCK:(k + 1) * BLOCK]
                parts.append(jnp.where(rows < limits_ref[g, t, c], block, FLOOR))
            pieces.append((parts, values))
        peak = None
        for parts, _ in pieces:
            for s in parts:
                top = jnp.max(s, axis=0, keepdims=True)
                peak = top if peak is None else jnp.maximum(peak, top)
        peak = peak * scale
        total = jnp.zeros((1, tok), jnp.float32)
        running = jnp.zeros((hd, tok), jnp.float32)
        for parts, values in pieces:
            weights = []
            for s in parts:
                w = jnp.exp2(s * scale - peak)
                total = total + jnp.sum(w, axis=0, keepdims=True)
                weights.append(w.astype(jnp.bfloat16))
            p = weights[0] if len(weights) == 1 else jnp.concatenate(weights, axis=0)
            running = running + jnp.dot(values, p, preferred_element_type=jnp.float32)
        return running / total, peak + jnp.log2(total)

    def merge(way, t, h):
        theirs, ours = lin[way, t, h], lacc[t, h]
        top = jnp.maximum(theirs, ours)
        a, b = jnp.exp2(theirs - top), jnp.exp2(ours - top)
        both = a + b
        mixed = rin[way, t, h].astype(jnp.float32) * (a / both) + acc[t, h] * (b / both)
        return mixed, top + jnp.log2(both)

    def emit(way, t, h, o, l):
        rout[t, h] = o.astype(jnp.bfloat16)
        lout[t, h] = l
        for copy in r_copies(way, t, h):
            copy.start()

    @pl.loop(0, heads)
    def _(h):
        o, l = partial(q_ref[h], me, h)
        acc[me, h] = o
        lacc[me, h] = l

    @pl.loop(1, n)
    def _(r):
        @pl.loop(0, heads)
        def _(h):
            for way in (0, 1):
                t = me - r if way == 0 else me + r
                there = t >= 0 if way == 0 else t < n

                @pl.when(there)
                def _():
                    q_copy(qbuf.at[t, h], way, t, h).wait_recv()

                    @pl.when(can_send(way))
                    def _():
                        q_copy(qbuf.at[t, h], way, t, h).start()

            for way in (0, 1):
                t = me - r if way == 0 else me + r
                there = t >= 0 if way == 0 else t < n

                @pl.when(there)
                def _():
                    o, l = partial(qbuf[t, h], t, h)

                    @pl.when(can_send(way))
                    def _():
                        acc[t, h] = o
                        lacc[t, h] = l

                    @pl.when(jnp.logical_not(can_send(way)))
                    def _():
                        emit(1 - way, t, h, o, l)

            for way in (0, 1):
                t = r if way == 0 else n - 1 - r
                inner = (me > 0) & (me < t) if way == 0 else (me < n - 1) & (me > t)

                @pl.when(inner)
                def _():
                    for copy in r_copies(way, t, h):
                        copy.wait_recv()
                    o, l = merge(way, t, h)
                    emit(way, t, h, o, l)

                @pl.when(me == t)
                def _():
                    for copy in r_copies(way, t, h):
                        copy.wait_recv()
                    o, l = merge(way, t, h)
                    acc[t, h] = o
                    lacc[t, h] = l

    @pl.loop(0, heads)
    def _(h):
        out_ref[h] = acc[me, h].T.astype(out_ref.dtype)
        for way in (0, 1):
            @pl.when(can_send(way))
            def _():
                q_copy(q_ref.at[h], way, me, h).wait_send()

        @pl.loop(0, n)
        def _(t):
            @pl.when(t != me)
            def _():
                for copy in r_copies(0, t, h):
                    copy.wait_send()

            @pl.when((t < me) & can_send(0))
            def _():
                q_copy(qbuf.at[t, h], 0, t, h).wait_send()

            @pl.when((t > me) & can_send(1))
            def _():
                q_copy(qbuf.at[t, h], 1, t, h).wait_send()


def shards(
    n, queries, new_keys, new_values, cache_keys, cache_values, block_slot, block_lists, frame_pos
):
    tok, heads, hd = queries.shape[1:]
    kv_heads = new_keys.shape[2]
    cb_dev = cache_keys.shape[1] // BLOCK
    capacity = min(cb_dev, max(2, -(-block_lists.shape[3] // n)))
    slots, limits = local_blocks(
        block_slot[0], block_lists[0], frame_pos[0], lax.axis_index("ctx"), cb_dev, capacity
    )
    q = jnp.transpose(queries[0], (1, 0, 2))
    kn = jnp.transpose(new_keys[0], (1, 0, 2))
    vn = jnp.transpose(new_values[0], (1, 2, 0))
    kc = jnp.transpose(cache_keys[0].reshape(cb_dev, BLOCK, kv_heads, hd), (2, 0, 1, 3))
    vc = jnp.transpose(cache_values[0].reshape(cb_dev, BLOCK, kv_heads, hd), (2, 0, 3, 1))
    smem = pl.BlockSpec(memory_space=pltpu.SMEM)
    vmem = pl.BlockSpec(memory_space=pltpu.VMEM)
    bf16, f32 = jnp.bfloat16, jnp.float32
    dma = pltpu.SemaphoreType.DMA
    out = pl.pallas_call(
        functools.partial(kernel, n),
        out_shape=jax.ShapeDtypeStruct((heads, tok, hd), bf16),
        in_specs=[smem, smem] + [vmem] * 5,
        out_specs=vmem,
        scratch_shapes=[
            pltpu.VMEM((n, heads, tok, hd), bf16),
            pltpu.VMEM((2, n, heads, hd, tok), bf16),
            pltpu.VMEM((2, n, heads, 1, tok), f32),
            pltpu.VMEM((n, heads, hd, tok), bf16),
            pltpu.VMEM((n, heads, 1, tok), f32),
            pltpu.VMEM((n, heads, hd, tok), f32),
            pltpu.VMEM((n, heads, 1, tok), f32),
            dma((2, n, heads)),
            dma((n, heads)),
            dma((n, heads)),
            dma((2, n, heads)),
            dma((n, heads)),
            dma((2, n, heads)),
        ],
        compiler_params=pltpu.CompilerParams(
            collective_id=0, has_side_effects=True, vmem_limit_bytes=56 * 1024 * 1024
        ),
    )(slots, limits, q, kn, vn, kc, vc)
    return jnp.transpose(out, (1, 0, 2))[None]


def solution(mesh):
    placed = (
        P(("groups", "stream"), "ctx", "head", None),
        P(("groups", "stream"), "ctx", "head", None),
        P(("groups", "stream"), "ctx", "head", None),
        P(("groups", "stream"), "ctx", "head", None),
        P(("groups", "stream"), "ctx", "head", None),
        P(("groups", "stream"), None),
        P(("groups", "stream"), "head", None, None),
        P(("groups", "stream")),
    )
    return jax.shard_map(
        functools.partial(shards, mesh.shape["ctx"]),
        mesh=mesh,
        in_specs=placed,
        out_specs=P(("groups", "stream"), "ctx", "head", None),
        check_vma=False,
    )
```

profile of v0, /device:TPU:0, one launch (start us, length us, event | category | flops | bytes accessed | tf_op | source)
XLA Modules:
  0.0 223.6 jit_solution(16497226454462487638)
XLA Ops:
  0.0 0.0 copy-start
  0.7 1.0 select_reduce_fusion
  1.8 0.7 add_select_fusion
  2.5 0.2 convert_reduce_fusion
  2.7 1.0 select_reduce_fusion.1
  3.7 1.7 copy.25
  5.3 1.8 copy.18
  7.2 0.0 copy-done
  7.2 0.0 copy-start.1
  7.2 1.0 copy.19
  8.2 0.4 copy-done.1
  8.6 1.8 copy.21
  10.4 211.1 %shard_map.82 = bf16[6,512,128]{2,1,0:T(8,128)(2,1)} custom-call(s32[2,4,8]{2,1,0:T(4,128)} %get-tuple-element.6.slots_ref, s32[2,4,8]{2,1,0:T(4,128)} %get-tuple-element.5.limits_ref, bf16[6,512,128]{2,1,0:T(8,128)(2,1)} %bitcast.29, bf16[2,512,128]{2,1,0:T(8,128)(2,1)} %bitcast.27, bf16[2,128,512]{2,1,0:T(8,128)(2,1)} %bitcast.28, ...), custom_call_target="tpu_custom_call" | custom-call | tf_op jit(solution)/shard_map/pallas_call | solution.py:239
  221.5 2.1 copy.28
  (2 shorter events, 0.0 us)
Async XLA Ops:
  0.0 7.2 %copy-start = (bf16[1,1536,2,128]{3,2,1,0:T(2,128)(2,1)S(1)}, bf16[1,1536,2,128]{3,2,1,0:T(2,128)(2,1)}, u32[]{:S(2)}) copy-start(bf16[1,1536,2,128]{3,2,1,0:T(2,128)(2,1)} %param.11) | copy-start | bytes 2359300
  7.2 1.4 copy-start.1
where the time goes:
time: 224 us
  Pallas kernels  211 us (94%)
  local copies, waits for them, and re-layouts  8.78 us (4%)
  other arithmetic  2.91 us (1%)
    pallas_call x1, Pallas kernels, shards(): pl.pallas_call(functools.partial(kernel, n), out_shape=jax.ShapeDtypeStru...  211 us
    unnamed x8, local copies, waits for them, and re-layouts  6.99 us

commit v1 on v0

--- a/solution.py
+++ b/solution.py
@@ -137,65 +137,83 @@
 
     @pl.loop(0, heads)
     def _(h):
-        o, l = partial(q_ref[h], me, h)
-        acc[me, h] = o
-        lacc[me, h] = l
-
-    @pl.loop(1, n)
-    def _(r):
-        @pl.loop(0, heads)
-        def _(h):
+        qbuf[me, h] = q_ref[h]
+
+    to_right = 2 * me < n - 1
+    shorter = jnp.where(to_right, me, n - 1 - me)
+    sign = jnp.where(to_right, 1, -1)
+    near_way = jnp.where(to_right, 0, 1)
+
+    def tile_of(k):
+        paired = k <= 2 * shorter
+        distance = jnp.where(paired, (k + 1) // 2, k - shorter)
+        side = jnp.where(paired & (k % 2 == 0), -sign, sign)
+        return jnp.where(k == n, me, me + side * distance)
+
+    def chain(way, r, h):
+        t = jnp.where(way == 0, r, n - 1 - r)
+        inner = jnp.where(way == 0, (me > 0) & (me < t), (me < n - 1) & (me > t))
+
+        @pl.when(inner)
+        def _():
+            for copy in r_copies(way, t, h):
+                copy.wait_recv()
+            o, l = merge(way, t, h)
+            emit(way, t, h, o, l)
+
+    @pl.loop(0, n * heads + 2)
+    def _(u):
+        k, h = u // heads + 1, u % heads
+
+        for way in (0, 1):
+            t = me - k if way == 0 else me + k
+
+            @pl.when((t >= 0) & (t < n) & (k < n))
+            def _():
+                q_copy(qbuf.at[t, h], way, t, h).wait_recv()
+
+                @pl.when(can_send(way))
+                def _():
+                    q_copy(qbuf.at[t, h], way, t, h).start()
+
+        @pl.when(k <= n)
+        def _():
+            t = tile_of(k)
+            o, l = partial(qbuf[t, h], t, h)
+            first = ((me == 0) | (me == n - 1)) & (k < n)
+
+            @pl.when(jnp.logical_not(first))
+            def _():
+                acc[t, h] = o
+                lacc[t, h] = l
+
+            @pl.when(first)
+            def _():
+                emit(near_way, t, h, o, l)
+
+        for way, lag in ((near_way, heads), (1 - near_way, heads + 1)):
+            v = u - lag
+
+            @pl.when((v >= 0) & (v < (n - 1) * heads))
+            def _():
+                chain(way, v // heads + 1, v % heads)
+
+        e = u - (n - 1) * heads - 2
+
+        @pl.when(e >= 0)
+        def _():
             for way in (0, 1):
-                t = me - r if way == 0 else me + r
-                there = t >= 0 if way == 0 else t < n
-
-                @pl.when(there)
+                @pl.when(can_send(1 - way))
                 def _():
-                    q_copy(qbuf.at[t, h], way, t, h).wait_recv()
-
-                    @pl.when(can_send(way))
-                    def _():
-                        q_copy(qbuf.at[t, h], way, t, h).start()
-
-            for way in (0, 1):
-                t = me - r if way == 0 else me + r
-                there = t >= 0 if way == 0 else t < n
-
-                @pl.when(there)
-                def _():
-                    o, l = partial(qbuf[t, h], t, h)
-
-                    @pl.when(can_send(way))
-                    def _():
-                        acc[t, h] = o
-                        lacc[t, h] = l
-
-                    @pl.when(jnp.logical_not(can_send(way)))
-                    def _():
-                        emit(1 - way, t, h, o, l)
-
-            for way in (0, 1):
-                t = r if way == 0 else n - 1 - r
-                inner = (me > 0) & (me < t) if way == 0 else (me < n - 1) & (me > t)
-
-                @pl.when(inner)
-                def _():
-                    for copy in r_copies(way, t, h):
+                    for copy in r_copies(way, me, e):
                         copy.wait_recv()
-                    o, l = merge(way, t, h)
-                    emit(way, t, h, o, l)
-
-                @pl.when(me == t)
-                def _():
-                    for copy in r_copies(way, t, h):
-                        copy.wait_recv()
-                    o, l = merge(way, t, h)
-                    acc[t, h] = o
-                    lacc[t, h] = l
+                    o, l = merge(way, me, e)
+                    acc[me, e] = o
+                    lacc[me, e] = l
+            out_ref[e] = acc[me, e].T.astype(out_ref.dtype)
 
     @pl.loop(0, heads)
     def _(h):
-        out_ref[h] = acc[me, h].T.astype(out_ref.dtype)
         for way in (0, 1):
             @pl.when(can_send(way))
             def _():

time: 224 us -> 103 us (0.46)
  Pallas kernels: 211 us -> 90.2 us
    pallas_call x1, Pallas kernels: 211 us -> 90.2 us  [shards(): pl.pallas_call(functools.partial(kernel, n), out_shape=jax.ShapeDtypeStru...]
where the time goes in v1:
time: 103 us
  Pallas kernels  90.2 us (88%)
  local copies, waits for them, and re-layouts  8.78 us (9%)
  other arithmetic  2.91 us (3%)
    pallas_call x1, Pallas kernels, shards(): pl.pallas_call(functools.partial(kernel, n), out_shape=jax.ShapeDtypeStru...  90.2 us
    unnamed x8, local copies, waits for them, and re-layouts  6.99 us

profile of v1, /device:TPU:0, one launch (start us, length us, event | category | flops | bytes accessed | tf_op | source)
XLA Modules:
  0.0 102.7 jit_solution(6912021481814902540)
XLA Ops:
  0.0 0.0 copy-start
  0.7 1.0 select_reduce_fusion
  1.8 0.7 add_select_fusion
  2.5 0.2 convert_reduce_fusion
  2.7 1.0 select_reduce_fusion.1
  3.7 1.7 %copy.25 = bf16[1,512,2,128]{3,1,2,0:T(8,128)(2,1)} copy(bf16[1,512,2,128]{3,2,1,0:T(2,128)(2,1)} %param.9) | data formatting | bytes 524288 | tf_op args[1]
  5.3 1.8 %copy.18 = bf16[1,512,2,128]{1,3,2,0:T(8,128)(2,1)} copy(bf16[1,512,2,128]{3,2,1,0:T(2,128)(2,1)} %param.10) | data formatting | bytes 524288 | tf_op args[2]
  7.2 0.0 copy-done
  7.2 0.0 copy-start.1
  7.2 1.0 copy.19
  8.2 0.4 copy-done.1
  8.6 1.8 %copy.21 = bf16[12,128,2,128]{1,3,0,2:T(8,128)(2,1)} copy(bf16[12,128,2,128]{3,2,1,0:T(2,128)(2,1)S(1)} %bitcast.30) | data formatting | bytes 1572864 | tf_op jit(solution)/shard_map/reshape;squeeze | solution.py:252
  10.4 90.2 %shard_map.82 = bf16[6,512,128]{2,1,0:T(8,128)(2,1)} custom-call(s32[2,4,8]{2,1,0:T(4,128)} %get-tuple-element.6.slots_ref, s32[2,4,8]{2,1,0:T(4,128)} %get-tuple-element.5.limits_ref, bf16[6,512,128]{2,1,0:T(8,128)(2,1)} %bitcast.29, bf16[2,512,128]{2,1,0:T(8,128)(2,1)} %bitcast.27, bf16[2,128,512]{2,1,0:T(8,128)(2,1)} %bitcast.28, ...), custom_call_target="tpu_custom_call" | custom-call | tf_op jit(solution)/shard_map/pallas_call | solution.py:257
  100.6 2.1 %copy.28 = bf16[1,512,6,128]{3,1,2,0:T(8,128)(2,1)} copy(bf16[1,512,6,128]{3,1,2,0:T(8,128)(2,1)} %bitcast.24) | data formatting | bytes 1572864
  (2 shorter events, 0.0 us)
Async XLA Ops:
  0.0 7.2 %copy-start = (bf16[1,1536,2,128]{3,2,1,0:T(2,128)(2,1)S(1)}, bf16[1,1536,2,128]{3,2,1,0:T(2,128)(2,1)}, u32[]{:S(2)}) copy-start(bf16[1,1536,2,128]{3,2,1,0:T(2,128)(2,1)} %param.11) | copy-start | bytes 2359300
  7.2 1.4 %copy-start.1 = (bf16[1,1536,2,128]{3,2,1,0:T(2,128)(2,1)S(1)}, bf16[1,1536,2,128]{3,2,1,0:T(2,128)(2,1)}, u32[]{:S(2)}) copy-start(bf16[1,1536,2,128]{3,2,1,0:T(2,128)(2,1)} %param.12) | copy-start | bytes 2359300

commit v2 on v1

--- a/solution.py
+++ b/solution.py
@@ -34,12 +34,13 @@
 
 
 def kernel(
-    n, slots_ref, limits_ref, q_ref, kn_ref, vn_ref, kc_ref, vc_ref, out_ref,
+    n, slots_ref, limits_ref, q_ref, ql_ref, qr_ref, kn_ref, vn_ref, kc_ref, vc_ref, out_ref,
     qbuf, rin, lin, rout, lout, acc, lacc, qs, qr, rs, rr, ls, lr,
 ):
     heads, tok, hd = q_ref.shape
     group = heads // kn_ref.shape[0]
     capacity = slots_ref.shape[2]
+    early = ql_ref.shape[0]
     me = lax.axis_index("ctx")
     scale = LOG2E * hd ** -0.5
 
@@ -78,7 +79,7 @@
     def can_send(way):
         return me < n - 1 if way == 0 else me > 0
 
-    @pl.loop(0, heads)
+    @pl.loop(early, heads)
     def _(h):
         for way in (0, 1):
             @pl.when(can_send(way))
@@ -139,6 +140,16 @@
     def _(h):
         qbuf[me, h] = q_ref[h]
 
+    @pl.loop(0, early)
+    def _(h):
+        @pl.when(me > 0)
+        def _():
+            qbuf[me - 1, h] = ql_ref[h]
+
+        @pl.when(me < n - 1)
+        def _():
+            qbuf[me + 1, h] = qr_ref[h]
+
     to_right = 2 * me < n - 1
     shorter = jnp.where(to_right, me, n - 1 - me)
     sign = jnp.where(to_right, 1, -1)
@@ -170,7 +181,9 @@
 
             @pl.when((t >= 0) & (t < n) & (k < n))
             def _():
-                q_copy(qbuf.at[t, h], way, t, h).wait_recv()
+                @pl.when((k > 1) | (h >= early))
+                def _():
+                    q_copy(qbuf.at[t, h], way, t, h).wait_recv()
 
                 @pl.when(can_send(way))
                 def _():
@@ -215,7 +228,7 @@
     @pl.loop(0, heads)
     def _(h):
         for way in (0, 1):
-            @pl.when(can_send(way))
+            @pl.when(can_send(way) & (h >= early))
             def _():
                 q_copy(q_ref.at[h], way, me, h).wait_send()
 
@@ -246,6 +259,10 @@
         block_slot[0], block_lists[0], frame_pos[0], lax.axis_index("ctx"), cb_dev, capacity
     )
     q = jnp.transpose(queries[0], (1, 0, 2))
+    early = heads // 2
+    rights = [(i, i + 1) for i in range(n - 1)]
+    q_left = lax.ppermute(q[:early], "ctx", rights)
+    q_right = lax.ppermute(q[:early], "ctx", [(b, a) for a, b in rights])
     kn = jnp.transpose(new_keys[0], (1, 0, 2))
     vn = jnp.transpose(new_values[0], (1, 2, 0))
     kc = jnp.transpose(cache_keys[0].reshape(cb_dev, BLOCK, kv_heads, hd), (2, 0, 1, 3))
@@ -257,7 +274,7 @@
     out = pl.pallas_call(
         functools.partial(kernel, n),
         out_shape=jax.ShapeDtypeStruct((heads, tok, hd), bf16),
-        in_specs=[smem, smem] + [vmem] * 5,
+        in_specs=[smem, smem] + [vmem] * 7,
         out_specs=vmem,
         scratch_shapes=[
             pltpu.VMEM((n, heads, tok, hd), bf16),
@@ -277,7 +294,7 @@
         compiler_params=pltpu.CompilerParams(
             collective_id=0, has_side_effects=True, vmem_limit_bytes=56 * 1024 * 1024
         ),
-    )(slots, limits, q, kn, vn, kc, vc)
+    )(slots, limits, q, q_left, q_right, kn, vn, kc, vc)
     return jnp.transpose(out, (1, 0, 2))[None]
 
 

time: 103 us -> 99.5 us (0.966)
  Pallas kernels: 90.2 us -> 79.5 us
  starting transfers between devices: 0 us -> 6.87 us
  local copies, waits for them, and re-layouts: 8.78 us -> 10.5 us
  other arithmetic: 2.91 us -> 1.52 us
    pallas_call x1, Pallas kernels: 90.2 us -> 79.5 us  [shards(): pl.pallas_call(functools.partial(kernel, n), out_shape=jax.ShapeDtypeStru...]
    ppermute x0 -> x2, starting transfers between devices: none -> 6.87 us  [the longest x1 5.58 us: shards(): q_left = lax.ppermute(q[:early], 'ctx', rights)]
    slice x0 -> x1, local copies, waits for them, and re-layouts: none -> 1.09 us  [shards(): q_left = lax.ppermute(q[:early], 'ctx', rights)]
    unnamed x8 -> x18, local copies, waits for them, and re-layouts: 6.99 us -> 7.64 us
  transfers between devices with their start and end apart: 0 -> 2, of which waited for: 0 -> 0; matrix products, arithmetic and copies ran while one was open for 0% -> 7% of each run, Pallas kernels for 0% -> 0%
where the time goes in v2:
time: 99.5 us; the launch traced here: 99.1 us
  Pallas kernels  79.5 us (80%)
  local copies, waits for them, and re-layouts  10.5 us (11%)
  starting transfers between devices  6.87 us (7%)
  other arithmetic  1.52 us (2%)
    pallas_call x1, Pallas kernels, shards(): pl.pallas_call(functools.partial(kernel, n), out_shape=jax.ShapeDtypeStru...  79.5 us
    unnamed x18, local copies, waits for them, and re-layouts  7.64 us
    ppermute x1, starting transfers between devices, shards(): q_left = lax.ppermute(q[:early], 'ctx', rights)  5.58 us
  transfers between devices with their start and end apart: 2, of which 0 were waited for; matrix products, arithmetic and copies ran while one was open for 7% of the time, Pallas kernels for 0%

profile of v2, /device:TPU:0, one launch (start us, length us, event | category | flops | bytes accessed | tf_op | source)
XLA Modules:
  0.0 99.1 jit_solution(1677664554776185224)
XLA Ops:
  0.0 0.0 copy-start
  0.0 1.1 %slice.5 = bf16[3,512,128]{2,1,0:T(8,128)(2,1)S(1)} slice(bf16[6,512,128]{2,1,0:T(8,128)(2,1)} %bitcast.27), slice={[0:3], [0:512], [0:128]} | slice | bytes 786432 | tf_op jit(solution)/shard_map/slice | solution.py:264
  1.1 1.3 %collective-permute-start.1 = (bf16[3,512,128]{2,1,0:T(8,128)(2,1)S(1)}, bf16[3,512,128]{2,1,0:T(8,128)(2,1)S(1)}, u32[]{:S(2)}, u32[]{:S(2)}) collective-permute-start(bf16[3,512,128]{2,1,0:T(8,128)(2,1)S(1)} %slice.5), channel_id=1, source_target_pairs={{4,0},{8,4},{12,8},{5,1},{9,5},{13,9},{6,2},{10,6},{14,10},{7,3},{... | collective-permute-start | bytes 1179656 | tf_op jit(solution)/shard_map/ppermute | solution.py:265
  2.4 5.6 %collective-permute-start = (bf16[3,512,128]{2,1,0:T(8,128)(2,1)S(1)}, bf16[3,512,128]{2,1,0:T(8,128)(2,1)S(1)}, u32[]{:S(2)}, u32[]{:S(2)}) collective-permute-start(bf16[3,512,128]{2,1,0:T(8,128)(2,1)S(1)} %slice.5), channel_id=1, source_target_pairs={{0,4},{4,8},{8,12},{1,5},{5,9},{9,13},{2,6},{6,10},{10,14},{3,7},{... | collective-permute-start | bytes 1179656 | tf_op jit(solution)/shard_map/ppermute | solution.py:264
  8.0 0.0 copy-start.5
  8.0 0.0 copy-start.6
  8.0 0.7 copy-done.5
  8.7 0.0 copy-done.6
  8.7 0.3 select_reduce_fusion
  9.0 0.2 convert_reduce_fusion
  9.9 0.0 copy-start.4
  9.9 1.7 %copy.25 = bf16[1,512,2,128]{3,1,2,0:T(8,128)(2,1)} copy(bf16[1,512,2,128]{3,2,1,0:T(2,128)(2,1)} %param.9) | data formatting | bytes 524288 | tf_op args[1]
  11.7 0.0 copy-done.4
  11.7 0.9 copy.18
  12.5 0.0 copy-done
  12.5 0.0 copy-start.1
  12.5 1.0 copy.19
  13.5 0.4 copy-done.1
  13.9 1.8 %copy.21 = bf16[12,128,2,128]{1,3,0,2:T(8,128)(2,1)} copy(bf16[12,128,2,128]{3,2,1,0:T(2,128)(2,1)S(1)} %bitcast.31) | data formatting | bytes 1572864 | tf_op jit(solution)/shard_map/reshape;squeeze | solution.py:269
  15.8 1.0 select_reduce_fusion.1
  16.7 0.0 collective-permute-done.1.qr_ref
  16.7 0.0 copy-start.2
  16.7 0.0 collective-permute-done.ql_ref
  16.7 0.0 copy-start.3
  16.7 0.8 copy-done.2
  17.5 0.1 copy-done.3
  17.6 79.5 %shard_map.82 = bf16[6,512,128]{2,1,0:T(8,128)(2,1)} custom-call(s32[2,4,8]{2,1,0:T(4,128)} %get-tuple-element.6.slots_ref, s32[2,4,8]{2,1,0:T(4,128)} %get-tuple-element.5.limits_ref, bf16[6,512,128]{2,1,0:T(8,128)(2,1)} %bitcast.28, bf16[3,512,128]{2,1,0:T(8,128)(2,1)} %copy-done.3, bf16[3,512,128]{2,1,0:T(8,128)(2,1)} %copy-done.2, ...), custom_call_target="tpu_custom_call" | custom-call | tf_op jit(solution)/shard_map/pallas_call | solution.py:274
  97.1 2.1 %copy.28 = bf16[1,512,6,128]{3,1,2,0:T(8,128)(2,1)} copy(bf16[1,512,6,128]{3,1,2,0:T(8,128)(2,1)} %bitcast.26) | data formatting | bytes 1572864
  (3 shorter events, 0.0 us)
Async XLA Ops:
  0.0 12.5 %copy-start = (bf16[1,1536,2,128]{3,2,1,0:T(2,128)(2,1)S(1)}, bf16[1,1536,2,128]{3,2,1,0:T(2,128)(2,1)}, u32[]{:S(2)}) copy-start(bf16[1,1536,2,128]{3,2,1,0:T(2,128)(2,1)} %param.11) | copy-start | bytes 2359300
  1.1 15.6 %collective-permute-start.1 = (bf16[3,512,128]{2,1,0:T(8,128)(2,1)S(1)}, bf16[3,512,128]{2,1,0:T(8,128)(2,1)S(1)}, u32[]{:S(2)}, u32[]{:S(2)}) collective-permute-start(bf16[3,512,128]{2,1,0:T(8,128)(2,1)S(1)} %slice.5), channel_id=1, source_target_pairs={{4,0},{8,4},{12,8},{5,1},{9,5},{13,9},{6,2},{10,6},{14,10},{7,3},{... | collective-permute-start | bytes 1179656 | tf_op jit(solution)/shard_map/ppermute | solution.py:265
  2.4 14.3 %collective-permute-start = (bf16[3,512,128]{2,1,0:T(8,128)(2,1)S(1)}, bf16[3,512,128]{2,1,0:T(8,128)(2,1)S(1)}, u32[]{:S(2)}, u32[]{:S(2)}) collective-permute-start(bf16[3,512,128]{2,1,0:T(8,128)(2,1)S(1)} %slice.5), channel_id=1, source_target_pairs={{0,4},{4,8},{8,12},{1,5},{5,9},{9,13},{2,6},{6,10},{10,14},{3,7},{... | collective-permute-start | bytes 1179656 | tf_op jit(solution)/shard_map/ppermute | solution.py:264
  8.0 0.7 copy-start.5
  8.0 0.7 copy-start.6
  9.9 1.7 %copy-start.4 = (bf16[1,512,2,128]{3,2,1,0:T(2,128)(2,1)S(1)}, bf16[1,512,2,128]{3,2,1,0:T(2,128)(2,1)}, u32[]{:S(2)}) copy-start(bf16[1,512,2,128]{3,2,1,0:T(2,128)(2,1)} %param.10) | copy-start | bytes 786436
  12.5 1.4 %copy-start.1 = (bf16[1,1536,2,128]{3,2,1,0:T(2,128)(2,1)S(1)}, bf16[1,1536,2,128]{3,2,1,0:T(2,128)(2,1)}, u32[]{:S(2)}) copy-start(bf16[1,1536,2,128]{3,2,1,0:T(2,128)(2,1)} %param.12) | copy-start | bytes 2359300
  16.7 0.8 copy-start.2
  16.7 0.9 copy-start.3

commit v3 on v2

--- a/solution.py
+++ b/solution.py
@@ -78,13 +78,6 @@
 
     def can_send(way):
         return me < n - 1 if way == 0 else me > 0
-
-    @pl.loop(early, heads)
-    def _(h):
-        for way in (0, 1):
-            @pl.when(can_send(way))
-            def _():
-                q_copy(q_ref.at[h], way, me, h).start()
 
     def partial(q, t, h):
         g = h // group
@@ -136,19 +129,34 @@
         for copy in r_copies(way, t, h):
             copy.start()
 
+    @pl.loop(0, early)
+    def _(h):
+        @pl.when(me > 0)
+        def _():
+            qbuf[me - 1, h] = ql_ref[h]
+
+            @pl.when(can_send(0))
+            def _():
+                q_copy(qbuf.at[me - 1, h], 0, me - 1, h).start()
+
+        @pl.when(me < n - 1)
+        def _():
+            qbuf[me + 1, h] = qr_ref[h]
+
+            @pl.when(can_send(1))
+            def _():
+                q_copy(qbuf.at[me + 1, h], 1, me + 1, h).start()
+
+    @pl.loop(early, heads)
+    def _(h):
+        for way in (0, 1):
+            @pl.when(can_send(way))
+            def _():
+                q_copy(q_ref.at[h], way, me, h).start()
+
     @pl.loop(0, heads)
     def _(h):
         qbuf[me, h] = q_ref[h]
-
-    @pl.loop(0, early)
-    def _(h):
-        @pl.when(me > 0)
-        def _():
-            qbuf[me - 1, h] = ql_ref[h]
-
-        @pl.when(me < n - 1)
-        def _():
-            qbuf[me + 1, h] = qr_ref[h]
 
     to_right = 2 * me < n - 1
     shorter = jnp.where(to_right, me, n - 1 - me)
@@ -179,16 +187,21 @@
         for way in (0, 1):
             t = me - k if way == 0 else me + k
 
-            @pl.when((t >= 0) & (t < n) & (k < n))
-            def _():
-                @pl.when((k > 1) | (h >= early))
-                def _():
-                    q_copy(qbuf.at[t, h], way, t, h).wait_recv()
+            @pl.when((t >= 0) & (t < n) & (k < n) & ((k > 1) | (h >= early)))
+            def _():
+                q_copy(qbuf.at[t, h], way, t, h).wait_recv()
 
                 @pl.when(can_send(way))
                 def _():
                     q_copy(qbuf.at[t, h], way, t, h).start()
 
+        for way, lag in ((near_way, heads), (1 - near_way, heads + 1)):
+            v = u - lag
+
+            @pl.when((v >= 0) & (v < (n - 1) * heads))
+            def _():
+                chain(way, v // heads + 1, v % heads)
+
         @pl.when(k <= n)
         def _():
             t = tile_of(k)
@@ -203,13 +216,6 @@
             @pl.when(first)
             def _():
                 emit(near_way, t, h, o, l)
-
-        for way, lag in ((near_way, heads), (1 - near_way, heads + 1)):
-            v = u - lag
-
-            @pl.when((v >= 0) & (v < (n - 1) * heads))
-            def _():
-                chain(way, v // heads + 1, v % heads)
 
         e = u - (n - 1) * heads - 2
 

time: 99.5 us -> 99.8 us (level)
  no operation moved by 1% of the time
where the time goes in v3:
time: 99.8 us; the launch traced here: 99.4 us
  Pallas kernels  79.8 us (80%)
  local copies, waits for them, and re-layouts  10.5 us (11%)
  starting transfers between devices  6.87 us (7%)
  other arithmetic  1.52 us (2%)
    pallas_call x1, Pallas kernels, shards(): pl.pallas_call(functools.partial(kernel, n), out_shape=jax.ShapeDtypeStru...  79.8 us
    unnamed x18, local copies, waits for them, and re-layouts  7.64 us
    ppermute x1, starting transfers between devices, shards(): q_left = lax.ppermute(q[:early], 'ctx', rights)  5.58 us
  transfers between devices with their start and end apart: 2, of which 0 were waited for; matrix products, arithmetic and copies ran while one was open for 7% of the time, Pallas kernels for 0%

profile of v3, /device:TPU:0, one launch (start us, length us, event | category | flops | bytes accessed | tf_op | source)
XLA Modules:
  0.0 99.4 jit_solution(2415961879007311628)
XLA Ops:
  0.0 0.0 copy-start
  0.0 1.1 %slice.5 = bf16[3,512,128]{2,1,0:T(8,128)(2,1)S(1)} slice(bf16[6,512,128]{2,1,0:T(8,128)(2,1)} %bitcast.27), slice={[0:3], [0:512], [0:128]} | slice | bytes 786432 | tf_op jit(solution)/shard_map/slice | solution.py:270
  1.1 1.3 %collective-permute-start.1 = (bf16[3,512,128]{2,1,0:T(8,128)(2,1)S(1)}, bf16[3,512,128]{2,1,0:T(8,128)(2,1)S(1)}, u32[]{:S(2)}, u32[]{:S(2)}) collective-permute-start(bf16[3,512,128]{2,1,0:T(8,128)(2,1)S(1)} %slice.5), channel_id=1, source_target_pairs={{4,0},{8,4},{12,8},{5,1},{9,5},{13,9},{6,2},{10,6},{14,10},{7,3},{... | collective-permute-start | bytes 1179656 | tf_op jit(solution)/shard_map/ppermute | solution.py:271
  2.4 5.6 %collective-permute-start = (bf16[3,512,128]{2,1,0:T(8,128)(2,1)S(1)}, bf16[3,512,128]{2,1,0:T(8,128)(2,1)S(1)}, u32[]{:S(2)}, u32[]{:S(2)}) collective-permute-start(bf16[3,512,128]{2,1,0:T(8,128)(2,1)S(1)} %slice.5), channel_id=1, source_target_pairs={{0,4},{4,8},{8,12},{1,5},{5,9},{9,13},{2,6},{6,10},{10,14},{3,7},{... | collective-permute-start | bytes 1179656 | tf_op jit(solution)/shard_map/ppermute | solution.py:270
  8.0 0.0 copy-start.5
  8.0 0.0 copy-start.6
  8.0 0.7 copy-done.5
  8.7 0.0 copy-done.6
  8.7 0.3 select_reduce_fusion
  9.0 0.2 convert_reduce_fusion
  9.9 0.0 copy-start.4
  9.9 1.7 %copy.25 = bf16[1,512,2,128]{3,1,2,0:T(8,128)(2,1)} copy(bf16[1,512,2,128]{3,2,1,0:T(2,128)(2,1)} %param.9) | data formatting | bytes 524288 | tf_op args[1]
  11.7 0.0 copy-done.4
  11.7 0.9 copy.18
  12.5 0.0 copy-done
  12.5 0.0 copy-start.1
  12.5 1.0 copy.19
  13.5 0.4 copy-done.1
  13.9 1.8 %copy.21 = bf16[12,128,2,128]{1,3,0,2:T(8,128)(2,1)} copy(bf16[12,128,2,128]{3,2,1,0:T(2,128)(2,1)S(1)} %bitcast.31) | data formatting | bytes 1572864 | tf_op jit(solution)/shard_map/reshape;squeeze | solution.py:275
  15.8 1.0 select_reduce_fusion.1
  16.7 0.0 collective-permute-done.1.qr_ref
  16.7 0.0 copy-start.2
  16.7 0.0 collective-permute-done.ql_ref
  16.7 0.0 copy-start.3
  16.7 0.8 copy-done.2
  17.5 0.1 copy-done.3
  17.6 79.8 %shard_map.82 = bf16[6,512,128]{2,1,0:T(8,128)(2,1)} custom-call(s32[2,4,8]{2,1,0:T(4,128)} %get-tuple-element.6.slots_ref, s32[2,4,8]{2,1,0:T(4,128)} %get-tuple-element.5.limits_ref, bf16[6,512,128]{2,1,0:T(8,128)(2,1)} %bitcast.28, bf16[3,512,128]{2,1,0:T(8,128)(2,1)} %copy-done.3, bf16[3,512,128]{2,1,0:T(8,128)(2,1)} %copy-done.2, ...), custom_call_target="tpu_custom_call" | custom-call | tf_op jit(solution)/shard_map/pallas_call | solution.py:280
  97.4 2.1 %copy.28 = bf16[1,512,6,128]{3,1,2,0:T(8,128)(2,1)} copy(bf16[1,512,6,128]{3,1,2,0:T(8,128)(2,1)} %bitcast.26) | data formatting | bytes 1572864
  (3 shorter events, 0.0 us)
Async XLA Ops:
  0.0 12.5 %copy-start = (bf16[1,1536,2,128]{3,2,1,0:T(2,128)(2,1)S(1)}, bf16[1,1536,2,128]{3,2,1,0:T(2,128)(2,1)}, u32[]{:S(2)}) copy-start(bf16[1,1536,2,128]{3,2,1,0:T(2,128)(2,1)} %param.11) | copy-start | bytes 2359300
  1.1 15.6 %collective-permute-start.1 = (bf16[3,512,128]{2,1,0:T(8,128)(2,1)S(1)}, bf16[3,512,128]{2,1,0:T(8,128)(2,1)S(1)}, u32[]{:S(2)}, u32[]{:S(2)}) collective-permute-start(bf16[3,512,128]{2,1,0:T(8,128)(2,1)S(1)} %slice.5), channel_id=1, source_target_pairs={{4,0},{8,4},{12,8},{5,1},{9,5},{13,9},{6,2},{10,6},{14,10},{7,3},{... | collective-permute-start | bytes 1179656 | tf_op jit(solution)/shard_map/ppermute | solution.py:271
  2.4 14.3 %collective-permute-start = (bf16[3,512,128]{2,1,0:T(8,128)(2,1)S(1)}, bf16[3,512,128]{2,1,0:T(8,128)(2,1)S(1)}, u32[]{:S(2)}, u32[]{:S(2)}) collective-permute-start(bf16[3,512,128]{2,1,0:T(8,128)(2,1)S(1)} %slice.5), channel_id=1, source_target_pairs={{0,4},{4,8},{8,12},{1,5},{5,9},{9,13},{2,6},{6,10},{10,14},{3,7},{... | collective-permute-start | bytes 1179656 | tf_op jit(solution)/shard_map/ppermute | solution.py:270
  8.0 0.7 copy-start.5
  8.0 0.7 copy-start.6
  9.9 1.7 %copy-start.4 = (bf16[1,512,2,128]{3,2,1,0:T(2,128)(2,1)S(1)}, bf16[1,512,2,128]{3,2,1,0:T(2,128)(2,1)}, u32[]{:S(2)}) copy-start(bf16[1,512,2,128]{3,2,1,0:T(2,128)(2,1)} %param.10) | copy-start | bytes 786436
  12.5 1.4 %copy-start.1 = (bf16[1,1536,2,128]{3,2,1,0:T(2,128)(2,1)S(1)}, bf16[1,1536,2,128]{3,2,1,0:T(2,128)(2,1)}, u32[]{:S(2)}) copy-start(bf16[1,1536,2,128]{3,2,1,0:T(2,128)(2,1)} %param.12) | copy-start | bytes 2359300
  16.7 0.8 copy-start.2
  16.7 0.9 copy-start.3
